TPU v7x, 32 devices: a whole 2x2x4 slice. The times are simulated.
32 devices in a mesh: ctx: 4 (over x, core), fsdp: 8 (over z, y).
Axes of the slice: x: 2, y: 2, z: 4, core: 2. Of those that a mesh axis runs over, the one named last changes fastest.
Arguments:
- hidden_in: bfloat16 [8, 1024, 1024], P('fsdp', 'ctx'), may hold values from -6 to 6
- positions: int32 [8, 1024], P('fsdp', 'ctx'), may hold values from 0 to 1023, as said below
- out_grad: bfloat16 [8, 1024, 1024], P('fsdp', 'ctx'), may hold values from -6 to 6
- attn_gain: bfloat16 [1024], P('fsdp'), may hold values from 0.5 to 1.5
- attn_shift: bfloat16 [1024], P('fsdp'), may hold values from -4 to 4
- in_weight: bfloat16 [1024, 3072], P('fsdp'), may hold values from -0.25 to 0.25
- in_bias: bfloat16 [3072], P('fsdp'), may hold values from -4 to 4
- proj_weight: bfloat16 [1024, 1024], P('fsdp'), may hold values from -1 to 1
- proj_bias: bfloat16 [1024], P('fsdp'), may hold values from -4 to 4
- mlp_gain: bfloat16 [1024], P('fsdp'), may hold values from 0.5 to 1.5
- mlp_shift: bfloat16 [1024], P('fsdp'), may hold values from -4 to 4
- up_weight: bfloat16 [1024, 4096], P('fsdp'), may hold values from -0.1875 to 0.1875
- up_bias: bfloat16 [4096], P('fsdp'), may hold values from -4 to 4
- down_weight: bfloat16 [4096, 1024], P('fsdp'), may hold values from -0.125 to 0.125
- down_bias: bfloat16 [1024], P('fsdp'), may hold values from -4 to 4
Outputs:
- block_out: bfloat16 [8, 1024, 1024], P('fsdp', 'ctx')
- input_grad: float32 [8, 1024, 1024], P('fsdp', 'ctx')
- attn_gain_grad: float32 [1024], P('fsdp')
- attn_shift_grad: float32 [1024], P('fsdp')
- in_weight_grad: float32 [1024, 3072], P('fsdp')
- in_bias_grad: float32 [3072], P('fsdp')
- proj_weight_grad: float32 [1024, 1024], P('fsdp')
- proj_bias_grad: float32 [1024], P('fsdp')
- mlp_gain_grad: float32 [1024], P('fsdp')
- mlp_shift_grad: float32 [1024], P('fsdp')
- up_weight_grad: float32 [1024, 4096], P('fsdp')
- up_bias_grad: float32 [4096], P('fsdp')
- down_weight_grad: float32 [4096, 1024], P('fsdp')
- down_bias_grad: float32 [1024], P('fsdp')
Inputs may be any that keep to these rules, and one draw needn't show every extreme that they name: Row s lists the positions in sequence s of the tokens stored along it: a permutation of 0 to 1023 made of runs of 128 consecutive positions that start at multiples of 128. The 256 entries held by one index of ctx are two such runs, blocks b and 7 - b for some b, in either order.
All inputs are finite; a program needn't handle non-finite values.
Results may differ from a plain program's by a relative error of at most 0.017.
Values may be sent and summed in bfloat16 or wider, within the bound.
A program may use at most 192 MiB of HBM per device.

v0:
```python
import math

import jax
import jax.numpy as jnp
import numpy as np
from jax import lax
from jax.experimental import pallas as pl
from jax.experimental.pallas import tpu as pltpu
from jax.sharding import PartitionSpec as P

HEADS = 16
HEAD_DIM = 64
ROT = 16
BLK = 128
EPS = 1e-05
MESH = pl.DeviceIdType.MESH
BF = jnp.bfloat16
F32 = jnp.float32
IN, PROJ, UP, DOWN, VEC, CROSS, PIECE = range(7)
PIECES = 2
NAMES = "ipudvefgh"
VROWS = 16
BOTH1 = (((1,), (1,)), ((), ()))
BOTH0 = (((0,), (0,)), ((), ()))


def dot(a, b):
    return jnp.dot(a, b, preferred_element_type=F32)


def dot11(a, b):
    return lax.dot_general(a, b, BOTH1, preferred_element_type=F32)


def dot00(a, b):
    return lax.dot_general(a, b, BOTH0, preferred_element_type=F32)


def mult(value, of):
    return pl.multiple_of(value, of)


def both(*conds):
    out = conds[0]
    for cond in conds[1:]:
        out = jnp.logical_and(out, cond)
    return out


class Sizes:
    def __init__(self, tokens, width, hidden, nctx, nshard):
        self.T = tokens
        self.N = tokens * nctx
        self.D = width
        self.H = hidden // nctx
        self.G = width // nctx
        self.nctx = nctx
        self.F = nshard
        self.A = nctx
        self.B = nshard // nctx
        self.R = width // nshard
        self.hc = hidden // nshard // nctx
        self.vector_rows = (1, 1, 1, 1, 1, 1, nctx, 3)
        self.packed = self.R % 128 == 0 and self.hc % 128 == 0
        half = self.hc // 2
        pieces = min(PIECES, self.R // 16)
        part = self.R // pieces
        more = pieces - 1
        self.pieces = (IN,) + tuple(range(PIECE, PIECE + more))
        self.buffer = ("i", "p", "u", "d", "v", "d") + ("i",) * more
        self.stride = (self.R, self.R, self.R, self.hc, VROWS, self.hc) + (self.R,) * more
        self.offset = (0, 0, 0, 0, 0, self.hc - half) + tuple(part * (i + 1) for i in range(more))
        self.rows = (part, self.R, self.R, self.hc - half, VROWS, half) + (part,) * more
        self.gather_rows = (self.R,) + self.rows[1:]
        self.cols = (3 * self.G, width, self.H, width, 128, width) + (3 * self.G,) * more
        self.units = (self.F, self.B, self.F, self.F, self.F, self.F) + (self.F,) * more
        self.types = (BF, BF, BF, BF, F32, BF) + (BF,) * more
        self.gathered = (IN, PROJ, UP, DOWN, CROSS) + ((VEC,) if self.packed else ())
        self.kinds = self.gathered + self.pieces[1:]
        self.NY = 1 if self.B == 2 else self.B + 1


def scratch_plan(s):
    N, D, G, H = s.N, s.D, s.G, s.H
    vm = pltpu.VMEM
    dma = pltpu.SemaphoreType.DMA
    plan = dict(
        Xs=vm((N, D), BF),
        Gs=vm((N, D), BF),
        Bs=vm((s.nctx * 8, D), jnp.int32),
        cos_st=vm((N, 128), F32),
        sin_st=vm((N, 128), F32),
        nb=vm((N, D), BF),
        A1=vm((N, D), BF),
        A2=vm((N, D), BF),
        S=vm((N, 4 * G), BF),
        dq=vm((N, G), F32),
        dk=vm((N, G), F32),
        dv=vm((N, G), F32),
        att_st=vm((N, G), BF),
        dj=vm((N, 3 * G), BF),
        act=vm((N, H), BF),
        gp=vm((N, H), BF),
        dl=vm((N, H), BF),
        Po=vm((N, D), BF),
        Pc=vm((N, D), BF),
        r1=vm((2, 2 * s.T, D), BF),
        r2=vm((2, s.T, D), BF),
        cs=vm((8, D), F32),
        xo=vm((s.T, D), BF),
        xg=vm((s.T, D), F32),
    )
    if s.packed:
        plan["vecs"] = vm((8, D), F32)
        plan["FV"] = vm((s.nctx * VROWS, 128), F32)
        plan["vtot"] = vm((VROWS, 128), F32)
        for i, count in enumerate(s.vector_rows):
            plan[f"vin{i}"] = vm((count * 128,), BF)
        plan["loc_v"] = dma((len(s.vector_rows),))
    A, B, F = s.A, s.B, s.F
    for kind in s.kinds:
        name = NAMES[kind]
        r, cl = s.rows[kind], s.cols[kind]
        dt = s.types[kind]
        if kind < CROSS:
            size = (s.units[kind] * s.stride[kind], cl)
            plan["W" + name] = vm(size, dt)
            plan["G" + name] = vm(size, dt)
        cross, proj = kind == CROSS, kind == PROJ
        per = 1 if cross or proj else A
        cols = B if cross else 1
        plan["Y" + name] = vm((s.NY * per * r, cl), dt)
        plan["Z" + name] = vm((A * B * r if kind == VEC else 3 * cols * r, cl), dt)
        along_y = per if B == 2 else 2 * per * B
        if kind in s.gathered:
            plan["az" + name] = dma(((2 if proj else A + 1) * cols,))
            plan["ay" + name] = dma((along_y,))
            plan["ar" + name] = dma((s.units[kind],))
        plan["ys" + name] = dma((along_y,))
        plan["yr" + name] = dma((along_y,))
        plan["zs" + name] = dma((A if kind == VEC else 3 * cols,))
        plan["zr" + name] = dma((A if kind == VEC else 3 * cols,))
    plan.update(
        xa_s=dma((3, 3)),
        xa_r=dma((3, s.nctx)),
        cr_s=dma((2, 3)),
        cr_r=dma((2, 3)),
        fa_s=dma((len(s.rows), 3)),
        fa_r=dma((len(s.rows), 3)),
        fa_l=dma((len(s.rows),)),
        loc=dma((16,)),
        loc_i=dma((3,)),
        loc_u=dma((s.F if s.packed else 1,)),
    )
    return plan


def kernel_body(s, names, *refs):
    n = dict(zip(names, refs))
    T, N, D, G, H, A, B, R = s.T, s.N, s.D, s.G, s.H, s.A, s.B, s.R
    c = lax.axis_index("ctx")
    f = lax.axis_index("fsdp")
    zi, yi = f // B, f % B
    sib_c = c + 1 - 2 * (c % 2)
    xn_c = (c + s.nctx // 2) % s.nctx
    xs_c = (sib_c + s.nctx // 2) % s.nctx
    sib, xn = (sib_c, f), (xn_c, f)
    edge = (zi < A - 1, zi > 0, yi < B - 1, yi > 0)
    hop = ((c, f + B), (c, f - B), (c, f + 1), (c, f - 1))

    def when(cond, fn):
        pl.when(cond)(fn)

    def rcopy(src, dst, ssem, rsem, dev):
        return pltpu.make_async_remote_copy(
            src_ref=src, dst_ref=dst, send_sem=ssem, recv_sem=rsem, device_id=dev, device_id_type=MESH
        )

    def rows(ref, start, size):
        return ref.at[pl.ds(mult(start, size), size)]

    W = [n.get("W" + x) for x in s.buffer]

    def has(kind, oz):
        return (oz == c) if kind == PROJ else (oz == oz)

    def wunit(ref, kind, oz, oy, sizes=s.rows):
        at = oy if kind == PROJ else oz * B + oy
        return rows(ref, at * s.stride[kind] + s.offset[kind], sizes[kind])

    def along_y(kind, oz, oy, d):
        per = 1 if kind in (PROJ, CROSS) else A
        at = 0 if per == 1 else oz
        return at if B == 2 else (d * per + at) * B + oy

    def ag_copy(kind, oz, oy, d):
        u = wunit(W[kind], kind, oz, oy, s.gather_rows)
        name = NAMES[kind]
        if d >= 2:
            send = n["ay" + name].at[along_y(kind, oz, oy, d - 2)]
        elif kind == PROJ:
            send = n["az" + name].at[d]
        else:
            at = oz if d == 0 else jnp.where(oz == zi, A, oz)
            send = n["az" + name].at[at + (oy * (A + 1) if kind == CROSS else 0)]
        return rcopy(u, u, send, n["ar" + name].at[oy if kind == PROJ else oz * B + oy], hop[d])

    def va_copy(source, oz):
        u = wunit(W[VEC], VEC, source, yi)
        return rcopy(
            u, u, n["azv"].at[oz], n["arv"].at[source * B + yi], (c, oz * B + yi)
        )

    def va_start():
        for oz in range(A):
            when(zi != oz, lambda oz=oz: va_copy(zi, oz).start())
        for d in (2, 3):
            when(edge[d], lambda d=d: ag_copy(VEC, zi, yi, d).start())

    def va_z():
        for i in range(1, A):
            oz = (zi + i) % A
            va_copy(oz, zi).wait_recv()
            for d in (2, 3):
                when(edge[d], lambda d=d, oz=oz: ag_copy(VEC, oz, yi, d).start())

    def va_drain():
        for oz in range(A):
            when(zi != oz, lambda oz=oz: va_copy(zi, oz).wait_send())
        for oz in range(A):
            for oy in range(B):
                when(both(oy <= yi, edge[2]), lambda oz=oz, oy=oy: ag_copy(VEC, oz, oy, 2).wait_send())
                when(both(oy >= yi, edge[3]), lambda oz=oz, oy=oy: ag_copy(VEC, oz, oy, 3).wait_send())

    def ag_start(kind):
        for d in range(4):
            when(both(has(kind, zi), edge[d]), lambda d=d: ag_copy(kind, zi, yi, d).start())

    def ag_z(kind, t):
        for i in range(B if kind == CROSS else 1):
            oy = (yi + i) % B if i else yi
            for sign, d in ((-1, 0), (1, 1)):
                oz = zi + sign * (1 + t)

                def go(oz=oz, d=d, oy=oy):
                    ag_copy(kind, oz, oy, d).wait_recv()
                    for dd in (d,) if kind == CROSS else (d, 2, 3):
                        when(edge[dd], lambda dd=dd: ag_copy(kind, oz, oy, dd).start())

                when(both(oz >= 0, oz < A, has(kind, oz)), go)

    def ag_y(kind):
        for t in range(B - 1):
            for zz in {PROJ: [c], CROSS: [zi]}.get(kind, list(range(A))):
                for sign, d in ((-1, 2), (1, 3)):
                    oy = yi + sign * (1 + t)

                    def go(oy=oy, d=d, zz=zz):
                        ag_copy(kind, zz, oy, d).wait_recv()
                        onward = ([d] if B > 2 else []) + ([0, 1] if kind == CROSS else [])
                        for dd in onward:
                            when(edge[dd], lambda dd=dd: ag_copy(kind, zz, oy, dd).start())

                    when(both(oy >= 0, oy < B), go)

    def ag_drain(kind):
        for oz in [c] if kind == PROJ else list(range(A)):
            for oy in range(B) if kind == CROSS else [yi]:
                when(both(oz <= zi, edge[0]), lambda oz=oz, oy=oy: ag_copy(kind, oz, oy, 0).wait_send())
                when(both(oz >= zi, edge[1]), lambda oz=oz, oy=oy: ag_copy(kind, oz, oy, 1).wait_send())
        for oz in {PROJ: [c], CROSS: [zi]}.get(kind, list(range(A))):
            for oy in range(B):
                when(both(oy <= yi, edge[2]), lambda oz=oz, oy=oy: ag_copy(kind, oz, oy, 2).wait_send())
                when(both(oy >= yi, edge[3]), lambda oz=oz, oy=oy: ag_copy(kind, oz, oy, 3).wait_send())

    XA = ((n["Xs"], T), (n["Gs"], T), (n["Bs"], 8))

    def xa_copy(arr, slot, which):
        ref, r = XA[arr]
        u = rows(ref, slot * r, r)
        return rcopy(u, u, n["xa_s"].at[arr, which], n["xa_r"].at[arr, slot], (xn, sib)[which != 0])

    def xa_start(arr):
        xa_copy(arr, c, 0).start()
        xa_copy(arr, c, 1).start()

    def xa_wait(arr, slot):
        xa_copy(arr, slot, 0).wait_recv()

    def xa_fwd(arr):
        xa_wait(arr, xn_c)
        xa_copy(arr, xn_c, 2).start()

    def xa_drain(arr):
        xa_copy(arr, c, 0).wait_send()
        xa_copy(arr, c, 1).wait_send()
        xa_copy(arr, xn_c, 2).wait_send()

    GR = [n.get("G" + x) for x in s.buffer]
    YB = [n.get("Y" + x) for x in NAMES]
    ZB = [n.get("Z" + x) for x in NAMES]

    def add_into(dst, src):
        dst[...] = (dst[...].astype(F32) + src[...].astype(F32)).astype(dst.dtype)

    def ry_slot(kind, zz, target, d, receiver):
        r = s.rows[kind]
        per = 1 if kind in (PROJ, CROSS) else A
        at = 0 if per == 1 else zz
        if B == 2:
            slot = 0
        elif d == 0:
            slot = target
        else:
            slot = jnp.where(receiver == target, B, target)
        return rows(YB[kind], (slot * per + at) * r, r)

    def ry_copy(kind, zz, target, d, receiver):
        at = along_y(kind, zz, target, d)
        return rcopy(
            wunit(GR[kind], kind, zz, target),
            ry_slot(kind, zz, target, d, receiver),
            n["ys" + NAMES[kind]].at[at],
            n["yr" + NAMES[kind]].at[at],
            hop[2 + d],
        )

    pair_z = zi + 1 - 2 * (zi % 2)
    far_z = (zi + A // 2) % A
    diag_z = (pair_z + A // 2) % A
    by_step = [diag_z, pair_z, far_z, zi]

    def ry_zz(kind):
        return {PROJ: [c], CROSS: [zi], VEC: [zi]}.get(kind, by_step)

    def ry_send(kind, t, zz):
        hi, lo = B - 1 - t, t
        when(yi == 0, lambda: ry_copy(kind, zz, hi, 0, yi + 1).start())
        when(yi == B - 1, lambda: ry_copy(kind, zz, lo, 1, yi - 1).start())

    def ry_recv(kind, t, zz):
        hi, lo = B - 1 - t, t
        for target, d, cond, onward in (
            (hi, 0, both(yi > 0, yi <= hi), both(yi > 0, yi < hi)),
            (lo, 1, both(yi < B - 1, yi >= lo), both(yi < B - 1, yi > lo)),
        ):

            def go(target=target, d=d):
                ry_copy(kind, zz, target, d, yi).wait_recv()
                add_into(wunit(GR[kind], kind, zz, target), ry_slot(kind, zz, target, d, yi))

            when(cond, go)
            if B > 2:
                when(
                    onward,
                    lambda target=target, d=d: ry_copy(
                        kind, zz, target, d, yi + 1 - 2 * d
                    ).start(),
                )

    def ry_drain(kind):
        for zz in {PROJ: [c], CROSS: [zi], VEC: [zi]}.get(kind, list(range(A))):
            for target in range(B):
                when(yi < target, lambda zz=zz, target=target: ry_copy(kind, zz, target, 0, yi + 1).wait_send())
                when(yi > target, lambda zz=zz, target=target: ry_copy(kind, zz, target, 1, yi - 1).wait_send())

    def rz_cols(kind):
        return [(yi + i) % B for i in range(B)] if kind == CROSS else [yi]

    def rz_slot(kind, which, col):
        r = s.rows[kind]
        return rows(ZB[kind], (which * B + col if kind == CROSS else which) * r, r)

    def rz_copy(kind, which, col):
        at = which * B + col if kind == CROSS else which
        return rcopy(
            wunit(GR[kind], kind, by_step[which], col),
            rz_slot(kind, which, col),
            n["zs" + NAMES[kind]].at[at],
            n["zr" + NAMES[kind]].at[at],
            (c, (pair_z, pair_z, far_z)[which] * B + yi),
        )

    def rz_take(kind, which, target, col):
        rz_copy(kind, which, col).wait_recv()
        add_into(wunit(GR[kind], kind, target, col), rz_slot(kind, which, col))

    def rz_pair(kind, which):
        def go():
            for col in rz_cols(kind):
                rz_copy(kind, which, col).start()

        when(has(kind, by_step[which]), go)

    def rz_far(kind):
        def go():
            for col in rz_cols(kind):
                rz_take(kind, 0, far_z, col)
                rz_copy(kind, 2, col).start()

        when(has(kind, far_z), go)

    def rz_sum(kind):
        def go():
            for col in rz_cols(kind):
                rz_take(kind, 1, zi, col)
                rz_take(kind, 2, zi, col)

        when(has(kind, zi), go)

    def rz_drain(kind):
        for which in range(3):

            def go(which=which):
                for col in rz_cols(kind):
                    rz_copy(kind, which, col).wait_send()

            when(has(kind, by_step[which]), go)

    def ry_first(kind):
        for t in range(B - 2):
            for zz in ry_zz(kind):
                if t:
                    ry_send(kind, t, zz)
                ry_recv(kind, t, zz)
        if B > 2:
            for zz in ry_zz(kind):
                ry_send(kind, B - 2, zz)

    def ry_start(kind):
        if kind in s.kinds:
            for zz in ry_zz(kind):
                ry_send(kind, 0, zz)

    def if_kind(kind, fn, *args):
        if kind in s.kinds:
            fn(kind, *args)

    def ry_unit(kind, i):
        if i == 0:
            ry_first(kind)
        ry_recv(kind, B - 2, by_step[i])
        if i < 2:
            rz_pair(kind, i)

    def vs_copy(source, target):
        return rcopy(
            rows(GR[VEC], target * B * VROWS, B * VROWS),
            rows(ZB[VEC], source * B * VROWS, B * VROWS),
            n["zsv"].at[target],
            n["zrv"].at[source],
            (c, target * B + yi),
        )

    def vs_start():
        for i in range(1, A):
            vs_copy(zi, (zi + i) % A).start()

    def vs_sum():
        mine = rows(GR[VEC], zi * B * VROWS, B * VROWS)
        for i in range(1, A):
            source = (zi + i) % A
            vs_copy(source, zi).wait_recv()
            add_into(mine, rows(ZB[VEC], source * B * VROWS, B * VROWS))

    def vs_drain():
        for i in range(1, A):
            vs_copy(zi, (zi + i) % A).wait_send()

    def ry_vec():
        ry_first(VEC)
        ry_recv(VEC, B - 2, zi)

    def ry_cross():
        ry_first(CROSS)
        ry_recv(CROSS, B - 2, zi)

    def ry_proj():
        ry_first(PROJ)
        ry_recv(PROJ, B - 2, c)
        rz_pair(PROJ, 0)
        rz_pair(PROJ, 1)

    def fa_has(kind, slot):
        return (zi == slot) if kind == PROJ else (c == c)

    def fa_dst(kind, slot):
        if kind == VEC:
            return rows(n["FV"], slot * VROWS, VROWS)
        if kind == PROJ:
            return n["out_p"]
        out = n["out_" + s.buffer[kind]]
        if s.buffer[kind] == "d":
            return rows(out, slot * s.hc + s.offset[kind], s.rows[kind])
        return out.at[slot, pl.ds(s.offset[kind], s.rows[kind])]

    def fa_copy(kind, slot, which):
        src = wunit(GR[kind], kind, zi, yi) if which < 2 else fa_dst(kind, slot)
        return rcopy(
            src, fa_dst(kind, slot), n["fa_s"].at[kind, which], n["fa_r"].at[kind, which], (sib, xn, sib)[which]
        )

    def fa_local(kind):
        return pltpu.make_async_copy(wunit(GR[kind], kind, zi, yi), fa_dst(kind, c), n["fa_l"].at[kind])

    def each(copies, what):
        for copy in copies:
            getattr(copy, what)()

    def fa_start(kind):
        def go():
            fa_copy(kind, c, 1).start()
            fa_copy(kind, c, 0).start()
            fa_local(kind).start()

        when(fa_has(kind, c), go)

    def fa_fwd(kind):
        def go():
            fa_copy(kind, xn_c, 1).wait_recv()
            fa_copy(kind, xn_c, 2).start()

        when(fa_has(kind, xn_c), go)

    def fa_end(kind):
        when(fa_has(kind, sib_c), lambda: fa_copy(kind, sib_c, 0).wait_recv())
        when(fa_has(kind, xs_c), lambda: fa_copy(kind, xs_c, 2).wait_recv())

        def own():
            fa_copy(kind, c, 1).wait_send()
            fa_copy(kind, c, 0).wait_send()
            fa_local(kind).wait()

        when(fa_has(kind, c), own)
        when(fa_has(kind, xn_c), lambda: fa_copy(kind, xn_c, 2).wait_send())

    PC = (n["Po"], n["Pc"])

    def cr_copy(arr, which, slot):
        if which < 2:
            return rcopy(
                rows(PC[arr], slot * T, T),
                n["r1"].at[arr, pl.ds(which * T, T)],
                n["cr_s"].at[arr, which],
                n["cr_r"].at[arr, which],
                sib,
            )
        return rcopy(rows(PC[arr], slot * T, T), n["r2"].at[arr], n["cr_s"].at[arr, 2], n["cr_r"].at[arr, 2], xn)

    def cr_start(arr):
        cr_copy(arr, 1, xs_c).start()
        cr_copy(arr, 0, sib_c).start()

    def cr_mid(arr):
        cr_copy(arr, 1, xs_c).wait_recv()
        add_into(rows(PC[arr], xn_c * T, T), n["r1"].at[arr, pl.ds(T, T)])
        cr_copy(arr, 2, xn_c).start()

    def cr_wait(arr):
        cr_copy(arr, 0, sib_c).wait_recv()
        cr_copy(arr, 2, xn_c).wait_recv()

    def cr_drain(arr):
        cr_copy(arr, 1, xs_c).wait_send()
        cr_copy(arr, 0, sib_c).wait_send()
        cr_copy(arr, 2, xn_c).wait_send()

    vecs, cos, sin = n["vecs"], n["cos"], n["sin"]

    def vec(row, width=D):
        return vecs[row : row + 1, 0:width]

    def loop(count, fn, first=0):
        def step(i, carry):
            fn(i)
            return carry

        lax.fori_loop(first, count, step, 0)

    def tile(ref, start, size, cols=slice(None)):
        return ref[pl.ds(mult(start, size), size), cols]

    def here(j, k, width):
        at = 8 * (j // 2) + j % 2
        return jnp.where(n["Bs"][at : at + 1, 0:width] == k, 1.0, 0.0)

    def to_order(dst, src):
        def one(k):
            total = None
            for j in range(2 * s.nctx):
                w = here(j, k, src.shape[1]).astype(src.dtype)
                term = src[j * BLK : (j + 1) * BLK, :] * w
                total = term if total is None else total + term
            dst[pl.ds(mult(k * BLK, BLK), BLK), :] = total

        loop(2 * s.nctx, one)

    def from_order(src, put):
        for j in range(2 * s.nctx):
            total = None
            for k in range(2 * s.nctx):
                w = here(j, k, src.shape[1]).astype(src.dtype)
                term = src[k * BLK : (k + 1) * BLK, :] * w
                total = term if total is None else total + term
            put(slice(j * BLK, (j + 1) * BLK), total)

    def norms(slot):
        def one(i):
            at = pl.ds(mult(slot * T + i * BLK, BLK), BLK)
            x = n["Xs"][at, :].astype(F32)
            center = x - jnp.mean(x, axis=-1, keepdims=True)
            nn = center * lax.rsqrt(jnp.mean(center * center, axis=-1, keepdims=True) + EPS)
            n["nb"][at, :] = nn.astype(BF)
            n["A1"][at, :] = (nn * vec(0) + vec(1)).astype(BF)
            n["A2"][at, :] = (nn * vec(2) + vec(3)).astype(BF)

        loop(T // BLK, one)

    lane64 = lax.broadcasted_iota(jnp.int32, (T, 128), 1) % HEAD_DIM
    first_half = lane64 < ROT // 2

    def rope(u, cs_, sn_, sign):
        partner = jnp.where(first_half, pltpu.roll(u, 128 - ROT // 2, 1), pltpu.roll(u, ROT // 2, 1))
        return u * cs_ + (partner * sn_) * sign

    def tables():
        def put(name):
            def store(at, value):
                n[name][at, :] = value

            return store

        from_order(cos, put("cos_st"))
        from_order(sin, put("sin_st"))

    raw, S = n["Pc"], n["S"]

    def qkv():
        def one(i):
            at = pl.ds(mult(i * T, T), T)
            j = dot(n["A1"][at, :], n["Wi"][...]) + vec(7, 3 * G)
            cs_, sn_ = n["cos_st"][at, :], n["sin_st"][at, :]
            for p in range(G // 128):
                lo = 128 * p
                q = rope(j[:, lo : lo + 128], cs_, sn_, 1.0).astype(BF)
                raw[at, lo : lo + 128] = (q.astype(F32) * HEAD_DIM**-0.5).astype(BF)
                raw[at, G + lo : G + lo + 128] = rope(j[:, G + lo : G + lo + 128], cs_, sn_, 1.0).astype(BF)
            raw[at, 2 * G : 3 * G] = j[:, 2 * G : 3 * G].astype(BF)

        loop(N // T, one)

    def dattended():
        def one(i):
            at = pl.ds(mult(i * T, T), T)
            raw[at, 3 * G : 4 * G] = dot11(n["Gs"][at, :], n["Wp"][...]).astype(BF)

        loop(N // T, one)

    def order():
        to_order(S, raw)

    def zero_dkv():
        n["dk"][...] = jnp.zeros((N, G), F32)
        n["dv"][...] = jnp.zeros((N, G), F32)

    def attention(p, i):
        L = (i + 1) * T
        cols = slice(128 * p, 128 * p + 128)
        at = slice(i * T, i * T + T)
        part = [slice(j * G + 128 * p, j * G + 128 * p + 128) for j in range(4)]
        kb, vb = S[0:L, part[1]], S[0:L, part[2]]
        qb, db = S[at, part[0]], S[at, part[3]]
        lane = lax.broadcasted_iota(jnp.int32, (T, 128), 1)
        key_at = lax.broadcasted_iota(jnp.int32, (T, T), 0)
        query_at = lax.broadcasted_iota(jnp.int32, (T, T), 1)
        keep = key_at <= query_at
        outs, dqs, ps, ds_, qs, dbs = [], [], [], [], [], []
        for h in range(2):
            mine = (lane >= HEAD_DIM) if h else (lane < HEAD_DIM)
            qh = jnp.where(mine, qb, jnp.zeros_like(qb))
            dh = jnp.where(mine, db, jnp.zeros_like(db))
            sc = dot11(kb, qh)
            last = jnp.where(keep, sc[L - T :], -1e30)
            sc = last if i == 0 else jnp.concatenate([sc[: L - T], last], axis=0)
            e = jnp.exp(sc - jnp.max(sc, axis=0, keepdims=True))
            pr = e * (1.0 / jnp.sum(e, axis=0, keepdims=True))
            dp = dot11(vb, dh)
            delta = jnp.sum(pr * dp, axis=0, keepdims=True)
            dsl = (pr * (dp - delta)).astype(BF)
            pb = pr.astype(BF)
            outs.append(dot00(vb, pb))
            dqs.append(dot00(kb, dsl))
            n["dv"][0:L, cols] += dot(pb, dh)
            n["dk"][0:L, cols] += dot(dsl, qh)
        feature = lax.broadcasted_iota(jnp.int32, (128, T), 0)
        raw[at, part[3]] = jnp.where(feature < HEAD_DIM, outs[0], outs[1]).T.astype(BF)
        n["dq"][at, cols] = jnp.where(feature < HEAD_DIM, dqs[0], dqs[1]).T * HEAD_DIM**-0.5

    def joined_back():
        n["cs"][2:3, :] = jnp.zeros((1, D), F32)

        def one(i):
            at = pl.ds(mult(i * T, T), T)
            cs_, sn_ = cos[at, :], sin[at, :]
            for p in range(G // 128):
                cols = slice(128 * p, 128 * p + 128)
                for j, (name, turn) in enumerate((("dq", True), ("dk", True), ("dv", False))):
                    u = n[name][at, cols]
                    if turn:
                        u = rope(u, cs_, sn_, -1.0)
                    u = u.astype(BF)
                    lo = j * G + 128 * p
                    raw[at, lo : lo + 128] = u
                    n["cs"][2:3, lo : lo + 128] += jnp.sum(u.astype(F32), axis=0, keepdims=True)

        loop(N // T, one)

        def put(at, value):
            n["dj"][at, :] = value[:, 0 : 3 * G]
            n["att_st"][at, :] = value[:, 3 * G : 4 * G]

        from_order(raw, put)

    def in_grad():
        def one(i):
            at = pl.ds(mult(i * 256, 256), 256)
            n["Gi"][at, :] = dot00(n["A1"][:, at], n["dj"][...]).astype(BF)

        loop(D // 256, one)

    def proj_grad():
        def one(i):
            at = pl.ds(mult(i * 256, 256), 256)
            n["Gp"][:, at] = dot00(n["att_st"][...], n["Gs"][:, at]).astype(BF)

        loop(D // 256, one)

    def mlp_up(part):
        def one(i):
            at = pl.ds(mult((i // 4) * T, T), T)
            cols = pl.ds(mult((i % 4) * 256, 256), 256)
            x = dot(n["A2"][at, :], n["Wu"][:, cols]) + vecs[6:7, cols]
            phi = 0.5 + 0.5 * lax.erf(x * math.sqrt(0.5))
            pdf = jnp.exp(-0.5 * x * x) * (1.0 / math.sqrt(2.0 * math.pi))
            n["act"][at, cols] = (x * phi).astype(BF)
            n["gp"][at, cols] = (phi + x * pdf).astype(BF)

        loop(4 * part + 4, one, 4 * part)

    def down_grad(part):
        def one(i):
            at = pl.ds(mult(i * 256, 256), 256)
            n["Gd"][at, :] = dot00(n["act"][:, at], n["Gs"][...]).astype(BF)

        loop(H // 512 * (part + 1), one, H // 512 * part)

    def mlp_back(part):
        if part == 0:
            n["cs"][6:7, :] = jnp.zeros((1, D), F32)

        def one(i):
            at = pl.ds(mult((i // 4) * T, T), T)
            cols = pl.ds(mult((i % 4) * 256, 256), 256)
            da = dot11(n["Gs"][at, :], n["Wd"][cols, :])
            dl = (da * n["gp"][at, cols].astype(F32)).astype(BF)
            n["dl"][at, cols] = dl
            n["cs"][6:7, cols] += jnp.sum(dl.astype(F32), axis=0, keepdims=True)

        loop(4 * part + 4, one, 4 * part)

    def up_grad(part):
        def one(i):
            at = pl.ds(mult(i * 256, 256), 256)
            n["Gu"][at, :] = dot00(n["A2"][:, at], n["dl"][...]).astype(BF)

        loop(D // 512 * (part + 1), one, D // 512 * part)

    def out_part():
        def one(i):
            at = pl.ds(mult(i * T, T), T)
            n["Po"][at, :] = (dot(n["att_st"][at, :], n["Wp"][...]) + dot(n["act"][at, :], n["Wd"][...])).astype(BF)

        loop(N // T, one)

    def input_part():
        for row in (0, 1, 4, 5):
            n["cs"][row : row + 1, :] = jnp.zeros((1, D), F32)

        def one(i):
            at = pl.ds(mult(i * T, T), T)
            nn = n["nb"][at, :].astype(F32)
            e1 = dot11(n["dj"][at, :], n["Wi"][...])
            n["cs"][0:1, :] += jnp.sum(e1 * nn, axis=0, keepdims=True)
            n["cs"][1:2, :] += jnp.sum(e1, axis=0, keepdims=True)
            e2 = dot11(n["dl"][at, :], n["Wu"][...])
            n["cs"][4:5, :] += jnp.sum(e2 * nn, axis=0, keepdims=True)
            n["cs"][5:6, :] += jnp.sum(e2, axis=0, keepdims=True)
            n["Pc"][at, :] = (e1 * vec(0) + e2 * vec(2)).astype(BF)

        loop(N // T, one)

    def own_g_sum():
        n["cs"][7:8, :] = jnp.zeros((1, D), F32)
        g = tile(n["Gs"], c * T, T).astype(F32)
        n["cs"][3:4, :] = jnp.sum(g, axis=0, keepdims=True)

    def finish_out():
        base = c * T
        x = tile(n["Xs"], base, T).astype(F32)
        total = tile(n["Po"], base, T).astype(F32) + n["r1"][0, 0:T].astype(F32) + n["r2"][0].astype(F32)
        n["xo"][...] = (x + total + vec(4) + vec(5)).astype(BF)

    def finish_input():
        base = c * T
        x = tile(n["Xs"], base, T).astype(F32)
        center = x - jnp.mean(x, axis=-1, keepdims=True)
        rstd = lax.rsqrt(jnp.mean(center * center, axis=-1, keepdims=True) + EPS)
        nn = center * rstd
        cc = tile(n["Pc"], base, T).astype(F32) + n["r1"][1, 0:T].astype(F32) + n["r2"][1].astype(F32)
        mean_c = jnp.mean(cc, axis=-1, keepdims=True)
        mean_cn = jnp.mean(cc * nn, axis=-1, keepdims=True)
        n["xg"][...] = tile(n["Gs"], base, T).astype(F32) + (cc - mean_c - nn * mean_cn) * rstd

    def unpack_vectors():
        for j in range(s.F):
            cols = slice(j * 128, (j + 1) * 128)
            n["vecs"][0:6, cols] = n["Wv"][j * VROWS : j * VROWS + 6, :]
            n["vecs"][6:7, cols] = n["Wv"][pl.ds(j * VROWS + 6 + c, 1), :]
        per = G // 128
        for j in range(3):
            for p in range(per):
                b = j * (D // 128) + c * per + p
                lo = (j * per + p) * 128
                n["vecs"][7:8, lo : lo + 128] = n["Wv"][pl.ds((b // 3) * VROWS + 6 + s.nctx + b % 3, 1), :]

    def pack_sums():
        n["Gv"][...] = jnp.zeros((s.F * VROWS, 128), F32)
        cs = n["cs"]
        for j in range(s.F):
            cols = slice(j * 128, (j + 1) * 128)
            base = j * VROWS
            for row, place in ((0, 0), (1, 1), (3, 5), (4, 6), (5, 7)):
                n["Gv"][base + place : base + place + 1, :] = cs[row : row + 1, cols]
            n["Gv"][pl.ds(base + 8 + c, 1), :] = cs[6:7, cols]
        per = G // 128
        for j in range(3):
            for p in range(per):
                b = j * (D // 128) + c * per + p
                lo = (j * per + p) * 128
                n["Gv"][pl.ds((b // 3) * VROWS + 2 + b % 3, 1), :] = cs[2:3, lo : lo + 128]

    def local(i, src, dst):
        return pltpu.make_async_copy(src, dst, n["loc"].at[i])

    own_i = rows(n["Wi"], (zi * B + yi) * R, R)
    own_u = wunit(W[UP], UP, zi, yi)
    hc = s.hc
    lc = {
        "x": [local(0, n["x"], rows(n["Xs"], c * T, T))],
        "i": [
            pltpu.make_async_copy(
                n["w_i"].at[:, pl.ds(mult(j * D + c * G, 128), G)], own_i.at[:, pl.ds(j * G, G)], n["loc_i"].at[j]
            )
            for j in range(3)
        ],
        "p": [local(3, n["w_p"], wunit(W[PROJ], PROJ, zi, yi))],
        "g": [local(4, n["g"], rows(n["Gs"], c * T, T))],
        "u": [local(5, n["w_u"], own_u)]
        if not s.packed
        else [
            pltpu.make_async_copy(
                n["w_u"].at[:, pl.ds(mult((j * s.nctx + c) * hc, 128), hc)],
                own_u.at[:, pl.ds(j * hc, hc)],
                n["loc_u"].at[j],
            )
            for j in range(s.F)
        ],
        "d": [local(6, rows(n["w_d"], c * hc, hc), rows(n["Wd"], (zi * B + yi) * hc, hc))],
    }
    if s.packed:
        lc["v"] = [
            pltpu.make_async_copy(n[f"vec{i}"], n[f"vin{i}"], n["loc_v"].at[i]) for i in range(len(s.vector_rows))
        ]

    def lstart(key):
        if key == "p":
            when(zi == c, lambda: each(lc[key], "start"))
        else:
            each(lc[key], "start")

    def lwait(key):
        if key == "p":
            when(zi == c, lambda: each(lc[key], "wait"))
        else:
            each(lc[key], "wait")

    for key in lc:
        lstart(key)
    bar = pltpu.get_barrier_semaphore()
    for dev in (sib, xn):
        pl.semaphore_signal(bar, inc=1, device_id=dev, device_id_type=MESH)
    for step in range(1, A):
        pl.semaphore_signal(bar, inc=1, device_id=(c, (zi + step) % A * B + yi), device_id_type=MESH)
    for d in (2, 3):
        when(
            edge[d],
            lambda d=d: pl.semaphore_signal(bar, inc=1, device_id=hop[d], device_id_type=MESH),
        )
    count = 2 + A - 1 + sum(jnp.where(e, 1, 0) for e in edge[2:])
    pl.semaphore_wait(bar, count)

    for key in lc:
        if key != "p":
            lwait(key)
    lwait("p")

    def blocks_start():
        for j in range(T // BLK):
            first = n["places"][0:1, j * BLK : j * BLK + 1] // BLK
            n["Bs"][pl.ds(c * 8 + j, 1), :] = jnp.broadcast_to(first, (1, D))
        xa_start(2)

    def vectors_start():
        if s.packed:
            at = (zi * B + yi) * VROWS
            for i, count in enumerate(s.vector_rows):
                for j in range(count):
                    n["Wv"][pl.ds(at, 1), :] = n[f"vin{i}"][j * 128 : (j + 1) * 128].astype(F32).reshape(1, 128)
                    at = at + 1
            va_start()

    def vectors_z():
        if s.packed:
            va_z()

    def vectors_y():
        if s.packed:
            ag_y(VEC)
            unpack_vectors()

    def sums_start():
        if s.packed:
            pack_sums()
            vs_start()

    def sums_y():
        if s.packed:
            vs_sum()
            ry_send(VEC, 0, zi)

    def sums_end():
        if s.packed:
            ry_vec()
            fa_start(VEC)

    def sums_fwd():
        if s.packed:
            fa_fwd(VEC)

    def cross_pair():
        rz_pair(CROSS, 0)
        rz_pair(CROSS, 1)

    def cross_y():
        rz_sum(CROSS)
        ry_send(CROSS, 0, zi)

    def cross_end():
        ry_cross()
        fa_start(CROSS)

    def done(kind):
        rz_sum(kind)
        fa_start(kind)

    put_out = local(12, n["xo"], n["out"])
    put_in = local(13, n["xg"], n["input_grad"])

    def store_out():
        cr_wait(0)
        finish_out()
        put_out.start()

    def store_input():
        cr_wait(1)
        finish_input()
        put_in.start()

    ag_start(IN)
    blocks_start()
    xa_start(0)
    own_g_sum()
    vectors_start()
    xa_wait(2, sib_c)
    xa_wait(0, sib_c)
    ag_start(PROJ)
    ag_z(IN, 0)
    zero_dkv()
    xa_start(1)
    vectors_z()
    xa_fwd(2)
    ag_z(PROJ, 0)
    xa_wait(2, xs_c)
    ag_z(IN, 1)
    xa_fwd(0)
    ag_start(UP)
    tables()
    ag_z(PROJ, 1)
    xa_wait(0, xs_c)
    xa_wait(1, sib_c)
    ag_z(IN, 2)
    ag_start(CROSS)
    vectors_y()
    norms(xs_c)
    norms(c)
    norms(sib_c)
    ag_z(PROJ, 2)
    ag_start(DOWN)
    xa_fwd(1)
    ag_z(UP, 0)
    norms(xn_c)
    xa_wait(1, xs_c)
    ag_y(IN)
    qkv()
    ag_y(PROJ)
    dattended()
    order()
    attention(0, 0)
    ag_z(UP, 1)
    ag_y(CROSS)
    attention(0, 1)
    ag_z(DOWN, 0)
    attention(0, 2)
    attention(0, 3)
    attention(1, 0)
    attention(1, 1)
    ag_z(UP, 2)
    attention(1, 2)
    attention(1, 3)
    ag_z(CROSS, 0)
    joined_back()
    ag_y(UP)
    mlp_up(0)
    ag_z(DOWN, 1)
    mlp_up(1)
    proj_grad()
    ag_z(CROSS, 1)
    ry_start(PROJ)
    mlp_up(2)
    ag_z(DOWN, 2)
    mlp_up(3)
    down_grad(0)
    down_grad(1)
    cross_pair()
    ag_z(CROSS, 2)
    in_grad()
    ag_y(DOWN)
    ry_start(DOWN)
    mlp_back(0)
    ry_proj()
    mlp_back(1)
    ry_start(PIECE)
    mlp_back(2)
    rz_far(CROSS)
    ry_unit(DOWN, 0)
    mlp_back(3)
    input_part()
    cr_start(1)
    if_kind(PIECE, ry_unit, 0)
    up_grad(0)
    if_kind(PIECE, ry_unit, 1)
    up_grad(1)
    ry_start(UP)
    rz_far(PROJ)
    cr_mid(1)
    ry_unit(DOWN, 1)
    sums_start()
    out_part()
    ry_unit(UP, 0)
    cr_start(0)
    ry_unit(DOWN, 2)
    done(PROJ)
    cross_y()
    rz_far(DOWN)
    cr_mid(0)
    ry_unit(UP, 1)
    ry_unit(UP, 2)
    rz_far(UP)
    ry_start(IN)
    ry_unit(DOWN, 3)
    sums_y()
    done(DOWN)
    if_kind(PIECE, ry_unit, 2)
    cross_end()
    ry_unit(UP, 3)
    ry_unit(IN, 0)
    if_kind(PIECE, rz_far)
    store_out()
    ry_unit(IN, 1)
    done(UP)
    ry_unit(IN, 2)
    rz_far(IN)
    sums_end()
    fa_fwd(PROJ)
    fa_fwd(DOWN)
    if_kind(PIECE, ry_unit, 3)
    fa_fwd(CROSS)
    if_kind(PIECE, done)
    ry_unit(IN, 3)
    done(IN)
    store_input()
    fa_fwd(UP)
    if_kind(PIECE, fa_fwd)
    fa_fwd(IN)
    sums_fwd()
    for kind in s.kinds:
        fa_end(kind)
    if s.packed:
        n["vtot"][...] = sum(n["FV"][j * VROWS : (j + 1) * VROWS, :] for j in range(s.nctx))
    put_cs = local(14, n["vtot"] if s.packed else n["cs"], n["sums"])
    put_cs.start()
    for kind in s.kinds:
        ry_drain(kind)
        if kind == VEC:
            va_drain()
            vs_drain()
        else:
            if kind in s.gathered:
                ag_drain(kind)
            rz_drain(kind)
    for arr in range(3):
        xa_drain(arr)
    for arr in range(2):
        cr_drain(arr)
    put_out.wait()
    put_in.wait()
    put_cs.wait()


def finish_kernel(s, hidden, *refs):
    gi, gp, gu, gd, out, input_grad, sums = refs[:7]
    to = refs[7:]
    to[0][...] = out[...]
    to[1][...] = input_grad[...]
    for slot in range(s.nctx):
        for j in range(3):
            lo = j * s.D + slot * s.G
            to[2][:, lo : lo + s.G] = gi[slot, :, j * s.G : (j + 1) * s.G].astype(F32)
        for j in range(s.F):
            lo = (j * s.nctx + slot) * s.hc
            to[4][:, lo : lo + s.hc] = gu[slot, :, j * s.hc : (j + 1) * s.hc].astype(F32)
    to[3][...] = gp[...].astype(F32)
    to[5][...] = gd[...].astype(F32)
    singles = ((0, 6), (1, 7), (5, 8), (6, 9), (7, 10), (5, 11))
    for row, at in singles:
        to[at][...] = sums[row, :]
    for first, count, at in ((2, 3, 12), (8, s.nctx, 13)):
        for j in range(count):
            to[at][j * 128 : (j + 1) * 128] = sums[first + j, :]


def finish(s, hidden, arrays):
    steps = max(1, s.R // 64)

    def part(shape):
        if len(shape) == 3:
            return pl.BlockSpec((shape[0], shape[1] // steps, shape[2]), lambda i: (0, i, 0))
        return pl.BlockSpec((shape[0] // steps, shape[1]), lambda i: (i, 0))

    def whole(shape):
        return pl.BlockSpec(shape, lambda i: (0,) * len(shape))

    D = s.D
    shapes = [(s.T, D), (s.T, D), (s.R, 3 * D), (s.R, D), (s.R, hidden), (hidden // s.F, D)]
    types = [BF, F32, F32, F32, F32, F32]
    small = [(128,)] * 6 + [(3 * s.R,), (hidden // s.F,)]
    return pl.pallas_call(
        lambda *refs: finish_kernel(s, hidden, *refs),
        grid=(steps,),
        out_shape=tuple(jax.ShapeDtypeStruct(sh, dt) for sh, dt in zip(shapes + small, types + [F32] * 8)),
        in_specs=[part(a.shape) for a in arrays[:-1]] + [whole(arrays[-1].shape)],
        out_specs=tuple([part(sh) for sh in shapes] + [whole(sh) for sh in small]),
        compiler_params=pltpu.CompilerParams(vmem_limit_bytes=63 << 20),
        name="finish",
    )(*arrays)


def rope_tables(length):
    half = ROT // 2
    freq = np.power(np.float32(10000.0), np.float32(-2.0) * np.arange(half, dtype=np.float32) / np.float32(ROT))
    angle = np.arange(length, dtype=np.float32)[:, None] * freq[None, :].astype(np.float32)
    cos = np.ones((length, 128), np.float32)
    sin = np.zeros((length, 128), np.float32)
    for base in range(0, 128, HEAD_DIM):
        cos[:, base : base + half] = np.cos(angle)
        cos[:, base + half : base + ROT] = np.cos(angle)
        sin[:, base : base + half] = -np.sin(angle)
        sin[:, base + half : base + ROT] = np.sin(angle)
    return cos, sin


def body(
    hidden_in,
    positions,
    out_grad,
    attn_gain,
    attn_shift,
    in_weight,
    in_bias,
    proj_weight,
    proj_bias,
    mlp_gain,
    mlp_shift,
    up_weight,
    up_bias,
    down_weight,
    down_bias,
):
    nctx, nshard = lax.axis_size("ctx"), lax.axis_size("fsdp")
    T, D = hidden_in.shape[1:]
    hidden = up_weight.shape[1]
    s = Sizes(T, D, hidden, nctx, nshard)
    R, G, F = s.R, s.G, s.F
    hc = s.hc
    c, f = lax.axis_index("ctx"), lax.axis_index("fsdp")

    def pick_ctx(array, axis):
        return lax.dynamic_index_in_dim(array, c, axis, keepdims=False)

    small = [attn_gain, attn_shift, mlp_gain, mlp_shift, proj_bias, down_bias, up_bias, in_bias]
    if s.packed:
        w_u = up_weight
        extra = {f"vec{i}": v for i, v in enumerate(small)}
    else:
        w_u = pick_ctx(up_weight.reshape(R, F, nctx, hc), 2).reshape(R, s.H)
        lengths = [v.shape[0] for v in small]
        gathered = lax.all_gather(jnp.concatenate(small).astype(F32), "fsdp", axis=0)
        full, at = [], 0
        for length in lengths:
            full.append(gathered[:, at : at + length].reshape(-1))
            at += length
        full[6] = pick_ctx(full[6].reshape(F, nctx, hc), 1).reshape(-1)
        full[7] = jnp.pad(pick_ctx(full[7].reshape(3, nctx, G), 1).reshape(-1), (0, D - 3 * G))
        extra = dict(vecs=jnp.stack(full))
    cos, sin = rope_tables(s.N)

    plan = scratch_plan(s)
    any_ = pl.BlockSpec(memory_space=pl.ANY)
    vmem = pl.BlockSpec(memory_space=pltpu.VMEM)
    ins = dict(
        x=hidden_in[0],
        g=out_grad[0],
        places=positions,
        w_i=in_weight,
        w_p=proj_weight,
        w_u=w_u,
        w_d=down_weight,
        **extra,
        cos=jnp.asarray(cos),
        sin=jnp.asarray(sin),
    )
    in_vmem = {"vecs", "cos", "sin", "places"}
    outs = dict(
        out=jax.ShapeDtypeStruct((T, D), BF),
        input_grad=jax.ShapeDtypeStruct((T, D), F32),
        out_i=jax.ShapeDtypeStruct((nctx, R, 3 * G), BF),
        out_p=jax.ShapeDtypeStruct((R, D), BF),
        out_u=jax.ShapeDtypeStruct((nctx, R, s.H), BF),
        out_d=jax.ShapeDtypeStruct((nctx * hc, D), BF),
        sums=jax.ShapeDtypeStruct((VROWS, 128) if s.packed else (8, D), F32),
    )
    names = list(ins) + list(outs) + list(plan)
    out, input_grad, gi, gp, gu, gd, sums = pl.pallas_call(
        lambda *refs: kernel_body(s, names, *refs),
        out_shape=tuple(outs.values()),
        in_specs=[vmem if name in in_vmem else any_ for name in ins],
        out_specs=tuple(any_ for _ in outs),
        scratch_shapes=list(plan.values()),
        compiler_params=pltpu.CompilerParams(
            collective_id=0, has_side_effects=True, vmem_limit_bytes=63 << 20
        ),
        name="block",
    )(*ins.values())

    def own(full_vector):
        length = full_vector.shape[0] // F
        return lax.dynamic_slice_in_dim(full_vector, f * length, length)

    if s.packed:
        done = finish(s, hidden, (gi, gp, gu, gd, out, input_grad, sums))
        out, input_grad, in_total, proj_total, up_total, down_total = done[:6]
        gain1, shift1, g_sum, gain2, shift2, g_again, in_bias_sum, up_bias_sum = done[6:]
    else:
        here = (jnp.arange(nctx) == c).astype(F32)
        in_b = (sums[2, : 3 * G].reshape(3, 1, G) * here[None, :, None]).reshape(-1)
        up_b = (sums[6].reshape(F, 1, hc) * here[None, :, None]).reshape(-1)
        total = lax.psum(
            jnp.concatenate([sums[0], sums[1], in_b, sums[3], sums[4], sums[5], up_b]), ("ctx", "fsdp")
        )
        parts, at = [], 0
        for length in (D, D, 3 * D, D, D, D, hidden):
            parts.append(own(total[at : at + length]))
            at += length
        gain1, shift1, in_bias_sum, g_sum, gain2, shift2, up_bias_sum = parts
        g_again = g_sum
        in_total = gi.astype(F32).reshape(nctx, R, 3, G).transpose(1, 2, 0, 3).reshape(R, 3 * D)
        proj_total, down_total = gp.astype(F32), gd.astype(F32)
        up_total = gu.astype(F32).reshape(nctx, R, F, hc).transpose(1, 2, 0, 3).reshape(R, hidden)
    return (
        out[None],
        input_grad[None],
        gain1,
        shift1,
        in_total,
        in_bias_sum,
        proj_total,
        g_sum,
        gain2,
        shift2,
        up_total,
        up_bias_sum,
        down_total,
        g_again,
    )


def solution(mesh):
    tok, vec, mat = P("fsdp", "ctx", None), P("fsdp"), P("fsdp", None)
    placed = (tok, P("fsdp", "ctx"), tok, vec, vec, mat, vec, mat, vec, vec, vec, mat, vec, mat, vec)
    return jax.shard_map(
        body,
        mesh=mesh,
        in_specs=placed,
        out_specs=(tok, tok, vec, vec, mat, vec, mat, vec, vec, vec, mat, vec, mat, vec),
        check_vma=False,
    )
```

profile of v0, /device:TPU:0, one launch (start us, length us, event | category | flops | bytes accessed | tf_op | source)
XLA Modules:
  0.0 151.6 jit_solution(3566452964897929277)
XLA Ops:
  0.7 145.6 %block.1 = (bf16[256,1024]{1,0:T(8,128)(2,1)}, f32[256,1024]{1,0:T(8,128)}, bf16[4,128,768]{2,1,0:T(8,128)(2,1)}, bf16[128,1024]{1,0:T(8,128)(2,1)}, bf16[4,128,...) custom-call(bf16[256,1024]{1,0:T(8,128)(2,1)} %bitcast.4, bf16[256,1024]{1,0:T(8,128)(2,1)} %bitcast.5, ...), custom_call_target="tpu_custom_call" | custom-call | tf_op jit(solution)/shard_map/block/pallas_call | solution.py:1273
  146.3 5.1 %finish.1 = (bf16[256,1024]{1,0:T(8,128)(2,1)}, f32[256,1024]{1,0:T(8,128)}, f32[128,3072]{1,0:T(8,128)}, f32[128,1024]{1,0:T(8,128)}, f32[128,4096]{1,0:T(8,128...) custom-call(bf16[4,128,768]{2,1,0:T(8,128)(2,1)} %get-tuple-element., ...), custom_call_target="tpu_custom_call" | custom-call | tf_op jit(solution)/shard_map/finish/pallas_call | solution.py:1177
where the time goes:
time: 152 us
  Pallas kernels  151 us (99%)
    pallas_call x1, Pallas kernels, body(): pl.pallas_call(lambda *refs: kernel_body(s, names, *refs), out_shape=tupl...  146 us
    pallas_call x1, Pallas kernels, finish(): pl.pallas_call(lambda *refs: finish_kernel(s, hidden, *refs), grid=(steps...  5.11 us

commit v1 on v0

--- a/solution.py
+++ b/solution.py
@@ -177,7 +177,7 @@
         )
 
     def rows(ref, start, size):
-        return ref.at[pl.ds(mult(start, size), size)]
+        return ref.at[pl.ds(mult(start, math.gcd(size, 64)), size)]
 
     W = [n.get("W" + x) for x in s.buffer]
 
@@ -986,131 +986,131 @@
         finish_input()
         put_in.start()
 
+    vectors_start()
+    own_g_sum()
     ag_start(IN)
+    xa_start(0)
+    ag_start(PROJ)
+    vectors_z()
     blocks_start()
-    xa_start(0)
-    own_g_sum()
-    vectors_start()
+    ag_z(IN, 0)
+    ag_z(PROJ, 0)
+    xa_start(1)
+    xa_fwd(0)
+    ag_z(IN, 1)
+    xa_wait(0, sib_c)
+    vectors_y()
+    norms(xn_c)
+    xa_fwd(2)
+    xa_wait(1, sib_c)
+    ag_z(PROJ, 1)
+    ag_z(IN, 2)
+    ag_start(CROSS)
+    xa_wait(2, xs_c)
+    zero_dkv()
+    xa_wait(0, xs_c)
+    norms(c)
     xa_wait(2, sib_c)
-    xa_wait(0, sib_c)
-    ag_start(PROJ)
-    ag_z(IN, 0)
-    zero_dkv()
-    xa_start(1)
-    vectors_z()
-    xa_fwd(2)
-    ag_z(PROJ, 0)
-    xa_wait(2, xs_c)
-    ag_z(IN, 1)
-    xa_fwd(0)
+    ag_z(PROJ, 2)
     ag_start(UP)
     tables()
-    ag_z(PROJ, 1)
-    xa_wait(0, xs_c)
-    xa_wait(1, sib_c)
-    ag_z(IN, 2)
-    ag_start(CROSS)
-    vectors_y()
+    norms(sib_c)
     norms(xs_c)
-    norms(c)
-    norms(sib_c)
-    ag_z(PROJ, 2)
+    xa_fwd(1)
     ag_start(DOWN)
-    xa_fwd(1)
-    ag_z(UP, 0)
-    norms(xn_c)
-    xa_wait(1, xs_c)
     ag_y(IN)
     qkv()
+    xa_wait(1, xs_c)
     ag_y(PROJ)
     dattended()
     order()
+    ag_z(UP, 0)
     attention(0, 0)
+    attention(0, 1)
+    attention(0, 2)
+    ag_y(CROSS)
+    attention(0, 3)
     ag_z(UP, 1)
-    ag_y(CROSS)
-    attention(0, 1)
-    ag_z(DOWN, 0)
-    attention(0, 2)
-    attention(0, 3)
     attention(1, 0)
     attention(1, 1)
+    attention(1, 2)
+    ag_z(CROSS, 0)
     ag_z(UP, 2)
-    attention(1, 2)
     attention(1, 3)
-    ag_z(CROSS, 0)
     joined_back()
-    ag_y(UP)
-    mlp_up(0)
-    ag_z(DOWN, 1)
-    mlp_up(1)
     proj_grad()
     ag_z(CROSS, 1)
     ry_start(PROJ)
+    ag_y(UP)
+    ag_z(DOWN, 0)
+    mlp_up(0)
+    mlp_up(1)
     mlp_up(2)
+    mlp_up(3)
+    ag_z(DOWN, 1)
+    down_grad(0)
+    ry_proj()
     ag_z(DOWN, 2)
-    mlp_up(3)
-    down_grad(0)
     down_grad(1)
     cross_pair()
     ag_z(CROSS, 2)
+    ry_start(DOWN)
+    ag_y(DOWN)
     in_grad()
-    ag_y(DOWN)
-    ry_start(DOWN)
+    out_part()
+    rz_far(PROJ)
     mlp_back(0)
-    ry_proj()
+    ry_unit(DOWN, 0)
     mlp_back(1)
+    mlp_back(2)
     ry_start(PIECE)
-    mlp_back(2)
+    cr_start(0)
+    mlp_back(3)
     rz_far(CROSS)
-    ry_unit(DOWN, 0)
-    mlp_back(3)
+    up_grad(0)
+    cr_mid(0)
+    up_grad(1)
+    ry_unit(DOWN, 1)
+    ry_start(UP)
+    if_kind(PIECE, ry_unit, 0)
+    if_kind(PIECE, ry_unit, 1)
+    ry_unit(DOWN, 2)
+    rz_far(DOWN)
     input_part()
+    ry_unit(UP, 0)
     cr_start(1)
-    if_kind(PIECE, ry_unit, 0)
-    up_grad(0)
-    if_kind(PIECE, ry_unit, 1)
-    up_grad(1)
-    ry_start(UP)
-    rz_far(PROJ)
+    done(PROJ)
+    if_kind(PIECE, ry_unit, 2)
+    if_kind(PIECE, rz_far)
     cr_mid(1)
-    ry_unit(DOWN, 1)
-    sums_start()
-    out_part()
-    ry_unit(UP, 0)
-    cr_start(0)
-    ry_unit(DOWN, 2)
-    done(PROJ)
-    cross_y()
-    rz_far(DOWN)
-    cr_mid(0)
+    ry_unit(DOWN, 3)
     ry_unit(UP, 1)
     ry_unit(UP, 2)
     rz_far(UP)
+    cross_y()
     ry_start(IN)
-    ry_unit(DOWN, 3)
-    sums_y()
     done(DOWN)
-    if_kind(PIECE, ry_unit, 2)
+    if_kind(PIECE, ry_unit, 3)
+    ry_unit(UP, 3)
     cross_end()
-    ry_unit(UP, 3)
+    sums_start()
     ry_unit(IN, 0)
-    if_kind(PIECE, rz_far)
-    store_out()
+    if_kind(PIECE, done)
     ry_unit(IN, 1)
     done(UP)
+    fa_fwd(DOWN)
     ry_unit(IN, 2)
     rz_far(IN)
+    sums_y()
+    ry_unit(IN, 3)
+    fa_fwd(PROJ)
+    store_input()
+    done(IN)
+    store_out()
     sums_end()
-    fa_fwd(PROJ)
-    fa_fwd(DOWN)
-    if_kind(PIECE, ry_unit, 3)
     fa_fwd(CROSS)
-    if_kind(PIECE, done)
-    ry_unit(IN, 3)
-    done(IN)
-    store_input()
+    if_kind(PIECE, fa_fwd)
     fa_fwd(UP)
-    if_kind(PIECE, fa_fwd)
     fa_fwd(IN)
     sums_fwd()
     for kind in s.kinds:

time: 152 us -> 149 us (0.980)
  Pallas kernels: 151 us -> 148 us
    pallas_call x1, Pallas kernels: 146 us -> 142 us  [body(): pl.pallas_call(lambda *refs: kernel_body(s, names, *refs), out_shape=tupl...]
where the time goes in v1:
time: 149 us; the launch traced here: 148 us
  Pallas kernels  148 us (99%)
    pallas_call x1, Pallas kernels, body(): pl.pallas_call(lambda *refs: kernel_body(s, names, *refs), out_shape=tupl...  142 us
    pallas_call x1, Pallas kernels, finish(): pl.pallas_call(lambda *refs: finish_kernel(s, hidden, *refs), grid=(steps...  5.11 us

profile of v1, /device:TPU:0, one launch (start us, length us, event | category | flops | bytes accessed | tf_op | source)
XLA Modules:
  0.0 148.4 jit_solution(6636706495714601912)
XLA Ops:
  0.7 142.4 %block.1 = (bf16[256,1024]{1,0:T(8,128)(2,1)}, f32[256,1024]{1,0:T(8,128)}, bf16[4,128,768]{2,1,0:T(8,128)(2,1)}, bf16[128,1024]{1,0:T(8,128)(2,1)}, bf16[4,128,...) custom-call(bf16[256,1024]{1,0:T(8,128)(2,1)} %bitcast.4, bf16[256,1024]{1,0:T(8,128)(2,1)} %bitcast.5, ...), custom_call_target="tpu_custom_call" | custom-call | tf_op jit(solution)/shard_map/block/pallas_call | solution.py:1273
  143.0 5.1 %finish.1 = (bf16[256,1024]{1,0:T(8,128)(2,1)}, f32[256,1024]{1,0:T(8,128)}, f32[128,3072]{1,0:T(8,128)}, f32[128,1024]{1,0:T(8,128)}, f32[128,4096]{1,0:T(8,128...) custom-call(bf16[4,128,768]{2,1,0:T(8,128)(2,1)} %get-tuple-element., ...), custom_call_target="tpu_custom_call" | custom-call | tf_op jit(solution)/shard_map/finish/pallas_call | solution.py:1177

commit v2 on v1

--- a/solution.py
+++ b/solution.py
@@ -1005,16 +1005,16 @@
     xa_wait(1, sib_c)
     ag_z(PROJ, 1)
     ag_z(IN, 2)
+    xa_wait(2, xs_c)
     ag_start(CROSS)
-    xa_wait(2, xs_c)
     zero_dkv()
     xa_wait(0, xs_c)
     norms(c)
     xa_wait(2, sib_c)
     ag_z(PROJ, 2)
     ag_start(UP)
+    norms(sib_c)
     tables()
-    norms(sib_c)
     norms(xs_c)
     xa_fwd(1)
     ag_start(DOWN)
@@ -1041,8 +1041,8 @@
     proj_grad()
     ag_z(CROSS, 1)
     ry_start(PROJ)
+    ag_z(DOWN, 0)
     ag_y(UP)
-    ag_z(DOWN, 0)
     mlp_up(0)
     mlp_up(1)
     mlp_up(2)
@@ -1082,8 +1082,8 @@
     done(PROJ)
     if_kind(PIECE, ry_unit, 2)
     if_kind(PIECE, rz_far)
+    ry_unit(DOWN, 3)
     cr_mid(1)
-    ry_unit(DOWN, 3)
     ry_unit(UP, 1)
     ry_unit(UP, 2)
     rz_far(UP)
@@ -1098,8 +1098,8 @@
     if_kind(PIECE, done)
     ry_unit(IN, 1)
     done(UP)
+    ry_unit(IN, 2)
     fa_fwd(DOWN)
-    ry_unit(IN, 2)
     rz_far(IN)
     sums_y()
     ry_unit(IN, 3)

time: 149 us -> 149 us (level)
  no operation moved by 1% of the time
where the time goes in v2:
time: 149 us; the launch traced here: 148 us
  Pallas kernels  148 us (99%)
    pallas_call x1, Pallas kernels, body(): pl.pallas_call(lambda *refs: kernel_body(s, names, *refs), out_shape=tupl...  142 us
    pallas_call x1, Pallas kernels, finish(): pl.pallas_call(lambda *refs: finish_kernel(s, hidden, *refs), grid=(steps...  5.11 us

profile of v2, /device:TPU:0, one launch (start us, length us, event | category | flops | bytes accessed | tf_op | source)
XLA Modules:
  0.0 148.4 jit_solution(15500344588274618786)
XLA Ops:
  0.7 142.4 %block.1 = (bf16[256,1024]{1,0:T(8,128)(2,1)}, f32[256,1024]{1,0:T(8,128)}, bf16[4,128,768]{2,1,0:T(8,128)(2,1)}, bf16[128,1024]{1,0:T(8,128)(2,1)}, bf16[4,128,...) custom-call(bf16[256,1024]{1,0:T(8,128)(2,1)} %bitcast.4, bf16[256,1024]{1,0:T(8,128)(2,1)} %bitcast.5, ...), custom_call_target="tpu_custom_call" | custom-call | tf_op jit(solution)/shard_map/block/pallas_call | solution.py:1273
  143.0 5.1 %finish.1 = (bf16[256,1024]{1,0:T(8,128)(2,1)}, f32[256,1024]{1,0:T(8,128)}, f32[128,3072]{1,0:T(8,128)}, f32[128,1024]{1,0:T(8,128)}, f32[128,4096]{1,0:T(8,128...) custom-call(bf16[4,128,768]{2,1,0:T(8,128)(2,1)} %get-tuple-element., ...), custom_call_target="tpu_custom_call" | custom-call | tf_op jit(solution)/shard_map/finish/pallas_call | solution.py:1177
